TPU v7x, 32 devices: a whole 2x2x4 slice. The times are simulated.
32 devices in a mesh: rep: 2 (over x), grp: 8 (over z, y), loc: 2 (over core).
Axes of the slice: x: 2, y: 2, z: 4, core: 2. Of those that a mesh axis runs over, the one named last changes fastest.
Arguments:
- moe_tokens: bfloat16 [128, 7168], P(('rep', 'grp', 'loc')), parts along dimension 0, may hold values from -6 to 6
- picked_groups: int32 [128, 4], P(('rep', 'grp', 'loc')), parts along dimension 0, may hold values from 0 to 7, all different within a row; in each aligned block of 4 rows (0 to 3, 4 to 7, ...) at most 3 rows name the same one
- gate_scores: float32 [128, 4], P(('rep', 'grp', 'loc')), parts along dimension 0, may hold values from 0.2 to 1.2
- w_gate: bfloat16 [8, 7168, 2048], P('grp', None, 'loc'), may hold values from -0.0625 to 0.0625
- w_up: bfloat16 [8, 7168, 2048], P('grp', None, 'loc'), may hold values from -0.0625 to 0.0625
- w_down: bfloat16 [8, 2048, 7168], P('grp', 'loc'), may hold values from -0.125 to 0.125
- query_latent: bfloat16 [64, 128, 512], P(('rep', 'grp', 'loc')), parts along dimension 0, may hold values from -9 to 9
- query_rope: bfloat16 [64, 8192], P(('rep', 'grp', 'loc')), parts along dimension 0, may hold values from -9 to 93
- cache_latent: bfloat16 [64, 2048, 512], P(('rep', 'grp', 'loc')), parts along dimension 0, may hold values from -6 to 6
- cache_rope: bfloat16 [64, 64, 2048], P(('rep', 'grp', 'loc')), parts along dimension 0, may hold values from -6 to 6
- cache_lengths: int32 [64], P(('rep', 'grp', 'loc')), parts along dimension 0, may hold values from 256 to 2048, as said below
Outputs:
- moe_out: bfloat16 [128, 7168], P(('rep', 'grp', 'loc')), parts along dimension 0
- attn_out: bfloat16 [64, 128, 512], P(('rep', 'grp', 'loc')), parts along dimension 0
There are 2 independent parts, one for each index of `rep`. A program takes and returns all parts, laid end to end along the dimension named above; an argument that names none is the same for every part. Nothing has to cross between parts.
Inputs may be any that keep to these rules, and one draw needn't show every extreme that they name: `picked_groups`: the 4 groups of a token differ; at most 3 of the 4 tokens of one device pick the same group, and in every draw some device has exactly 3 tokens for some group. `cache_lengths`: in every draw some request has all 2048 positions.
All inputs are finite; a program needn't handle non-finite values.
Results may differ from a plain program's by a relative error of at most 0.0066.
Values may be sent and summed in bfloat16 or wider, within the bound.
A program may use at most 128 MiB of HBM per device.

v0:
```python
import jax
import jax.numpy as jnp
from jax import lax
from jax.sharding import PartitionSpec as P

softmax_scale = 192.0 ** (-0.5)
mask_fill = -1e30


def expert_partial(row_block, gate_matrix, up_matrix, down_matrix):
    row_shape = row_block.shape
    flat_rows = row_block.reshape(-1, row_shape[-1])
    gate_pre = jnp.dot(flat_rows, gate_matrix, preferred_element_type=jnp.float32)
    up_pre = jnp.dot(flat_rows, up_matrix, preferred_element_type=jnp.float32)
    hidden_act = (jax.nn.silu(gate_pre) * up_pre).astype(jnp.bfloat16)
    return jnp.dot(hidden_act, down_matrix, preferred_element_type=jnp.float32).reshape(row_shape)


def attend_local(query_latent, query_rope, cache_latent, cache_rope, cache_lengths):
    requests = query_latent.shape[0]
    head_count = query_latent.shape[1]
    rotary_width = cache_rope.shape[1]
    rotary_query = query_rope.reshape(requests, head_count, rotary_width)
    scores = jnp.einsum(
        "bhq,blq->bhl", query_latent, cache_latent, preferred_element_type=jnp.float32
    )
    scores = scores + jnp.einsum(
        "bhr,brl->bhl", rotary_query, cache_rope, preferred_element_type=jnp.float32
    )
    scores = scores * softmax_scale
    positions = lax.broadcasted_iota(jnp.int32, (1, 1, cache_latent.shape[1]), 2)
    scores = jnp.where(positions < cache_lengths[:, None, None], scores, mask_fill)
    row_max = jnp.max(scores, axis=2, keepdims=True)
    exp_scores = jnp.exp(scores - row_max)
    weights = (exp_scores / jnp.sum(exp_scores, axis=2, keepdims=True)).astype(jnp.bfloat16)
    return jnp.einsum(
        "bhl,blq->bhq", weights, cache_latent, preferred_element_type=jnp.float32
    ).astype(jnp.bfloat16)


def shards(
    moe_tokens,
    picked_groups,
    gate_scores,
    w_gate,
    w_up,
    w_down,
    query_latent,
    query_rope,
    cache_latent,
    cache_rope,
    cache_lengths,
):
    attn_out = attend_local(query_latent, query_rope, cache_latent, cache_rope, cache_lengths)
    groups = lax.axis_size("grp")
    tok_count = moe_tokens.shape[0]
    model_width = moe_tokens.shape[1]
    group_iota = lax.broadcasted_iota(jnp.int32, (1, 1, groups), 2)
    pick_hits = picked_groups[:, :, None] == group_iota
    chosen = jnp.sum(pick_hits.astype(jnp.int32), axis=1)
    pick_weight = jnp.sum(jnp.where(pick_hits, gate_scores[:, :, None], 0.0), axis=1)
    slot_number = jnp.cumsum(chosen, axis=0) - chosen
    slot_iota = lax.broadcasted_iota(jnp.int32, (1, 1, tok_count), 2)
    placed = (slot_number[:, :, None] == slot_iota) & (chosen[:, :, None] > 0)
    send_rows = jnp.einsum(
        "tgc,td->gcd", placed.astype(jnp.bfloat16), moe_tokens, preferred_element_type=jnp.float32
    ).astype(jnp.bfloat16)
    gate_matrix = w_gate[0]
    up_matrix = w_up[0]
    down_matrix = w_down[0]
    loc_count = lax.axis_size("loc")
    spread = jnp.broadcast_to(send_rows[:, None], (groups, loc_count, tok_count, model_width))
    spread = spread.reshape(groups * loc_count, tok_count, model_width)
    partial_value = expert_partial(
        lax.all_to_all(spread, ("grp", "loc"), split_axis=0, concat_axis=0, tiled=True),
        gate_matrix,
        up_matrix,
        down_matrix,
    ).astype(jnp.bfloat16)
    returned = lax.all_to_all(
        partial_value, ("grp", "loc"), split_axis=0, concat_axis=0, tiled=True
    )
    returned = returned.reshape(groups, loc_count, returned.shape[1], model_width)
    results = jnp.sum(returned, axis=1, dtype=jnp.float32).astype(jnp.bfloat16)
    weighted = jnp.where(placed, pick_weight[:, :, None], 0.0)
    combined = jnp.einsum(
        "tgc,gcd->td", weighted, results.astype(jnp.float32), precision=lax.Precision.HIGHEST
    )
    moe_out = combined.astype(jnp.bfloat16)
    return (moe_out, attn_out)


def solution(mesh):
    placed = (
        P(("rep", "grp", "loc"), None),
        P(("rep", "grp", "loc"), None),
        P(("rep", "grp", "loc"), None),
        P("grp", None, "loc"),
        P("grp", None, "loc"),
        P("grp", "loc", None),
        P(("rep", "grp", "loc"), None, None),
        P(("rep", "grp", "loc"), None),
        P(("rep", "grp", "loc"), None, None),
        P(("rep", "grp", "loc"), None, None),
        P(("rep", "grp", "loc")),
    )
    return jax.shard_map(
        shards,
        mesh=mesh,
        in_specs=placed,
        out_specs=(P(("rep", "grp", "loc"), None), P(("rep", "grp", "loc"), None, None)),
        check_vma=False,
    )
```

profile of v0, /device:TPU:0, one launch (start us, length us, event | category | flops | bytes accessed | tf_op | source)
XLA Modules:
  0.0 85.8 jit_solution(10492471268651673871)
XLA Ops:
  0.6 0.0 copy-start
  0.6 0.8 convert_reduce_fusion
  1.5 1.2 %convolution_convert_fusion = bf16[8,4,7168]{2,0,1:T(8,128)(2,1)S(1)} fusion(bf16[4,7168]{1,0:T(4,128)(2,1)} %param.11, s32[4,8]{1,0:T(4,128)S(1)} %sub.15, pred[4,8]{1,0:T(4,128)(4,1)S(1)} %broadcast_compare_fusion), kind=kOutput, calls=%fused_computation.8 | convolution fusion | flops 2064640 | bytes 516256 | tf_op jit(solution)/shard_map/tgc,td->gcd/dot_general | solution.py:65
  2.7 0.0 copy-start.3
  2.7 0.0 copy-start.4
  2.7 0.0 copy-start.5
  2.7 0.4 copy.28
  3.1 1.2 %broadcast_in_dim.54 = bf16[8,2,4,7168]{3,2,1,0:T(4,128)(2,1)} broadcast(bf16[8,4,7168]{2,1,0:T(4,128)(2,1)S(1)} %copy.28), dimensions={0,2,3} | broadcast | bytes 1376256 | tf_op jit(solution)/shard_map/broadcast_in_dim | solution.py:72
  4.3 0.0 slice-start
  4.3 7.6 %all-to-all-start = ((bf16[16,4,7168]{2,1,0:T(4,128)(2,1)}), bf16[16,4,7168]{2,1,0:T(4,128)(2,1)}, u32[]{:S(2)}, u32[]{:S(2)}) async-start(bf16[16,4,7168]{2,1,0:T(4,128)(2,1)} %bitcast.1), calls=%async_computation | async-start | bytes 1835008 | tf_op jit(solution)/shard_map/all_to_all | solution.py:75
  11.9 0.0 copy-done.3
  11.9 0.7 reshape.61
  12.6 0.0 copy-done.4
  12.6 0.0 copy-done.5
  12.6 0.1 select_reduce_fusion
  12.7 20.0 %all-to-all-done = bf16[16,4,7168]{2,1,0:T(4,128)(2,1)} async-done(((bf16[16,4,7168]{2,1,0:T(4,128)(2,1)}), bf16[16,4,7168]{2,1,0:T(4,128)(2,1)}, u32[]{:S(2)}, u32[]{:S(2)}) %all-to-all-start) | async-done | bytes 917536 | tf_op jit(solution)/shard_map/all_to_all | solution.py:75
  32.8 1.7 %reshape.59 = bf16[64,7168]{1,0:T(8,128)(2,1)S(1)} reshape(bf16[16,4,7168]{2,1,0:T(4,128)(2,1)} %all-to-all-done) | data formatting | bytes 1835008 | tf_op jit(solution)/shard_map/reshape | solution.py:12
  34.4 0.0 slice-start.1
  34.4 0.0 slice-start.2
  34.5 0.0 slice-start.3
  34.5 8.0 %fusion.5 = f32[64,1024]{1,0:T(8,128)S(1)} fusion(bf16[64,7168]{1,0:T(8,128)(2,1)S(1)} %reshape.59, bf16[1,7168,1024]{2,1,0:T(8,128)(2,1)} %param.14), kind=kOutput, calls=%fused_computation.5 | convolution fusion | flops 939524096 | bytes 15859712 | tf_op jit(solution)/shard_map/dot_general | solution.py:13
  42.5 0.0 slice-done
  42.5 0.0 slice-done.1
  42.5 0.0 slice-done.2
  42.5 0.8 slice-done.3
  43.3 3.3 %fusion.18 = bf16[64,1024]{1,0:T(8,128)(2,1)} fusion(bf16[64,7168]{1,0:T(8,128)(2,1)S(1)} %reshape.59, bf16[1,7168,1024]{2,1,0:T(8,128)(2,1)S(1)} %bitcast.36, f32[64,1024]{1,0:T(8,128)S(1)} %fusion.5), kind=kOutput, calls=%fused_computation.19 | convolution fusion | flops 939917312 | bytes 15990784 | tf_op jit(solution)/shard_map/dot_general | solution.py:14
  46.6 1.0 %dot_general.29 = bf16[16,4,1024]{2,1,0:T(4,128)(2,1)S(1)} reshape(bf16[64,1024]{1,0:T(8,128)(2,1)} %fusion.18) | data formatting | bytes 262144 | tf_op jit(solution)/shard_map/dot_general | solution.py:16
  47.6 7.8 %fusion.7 = bf16[16,4,7168]{2,0,1:T(8,128)(2,1)S(1)} fusion(bf16[1,1024,7168]{2,1,0:T(8,128)(2,1)} %param.16, bf16[16,4,1024]{2,1,0:T(4,128)(2,1)S(1)} %dot_general.29), kind=kOutput, calls=%fused_computation.7 | convolution fusion | flops 939982848 | bytes 15728640 | tf_op jit(solution)/shard_map/dot_general | solution.py:16
  55.4 0.0 copy-start.2
  55.4 1.6 %copy.30 = bf16[16,4,7168]{2,1,0:T(4,128)(2,1)} copy(bf16[16,4,7168]{2,0,1:T(8,128)(2,1)S(1)} %fusion.7) | data formatting | bytes 1835008 | tf_op jit(solution)/shard_map/convert_element_type | solution.py:79
  57.0 0.0 copy-start.6
  57.0 6.3 %all-to-all-start.1 = ((bf16[16,4,7168]{2,1,0:T(4,128)(2,1)}), bf16[16,4,7168]{2,1,0:T(4,128)(2,1)S(1)}, u32[]{:S(2)}, u32[]{:S(2)}) async-start(bf16[16,4,7168]{2,1,0:T(4,128)(2,1)} %copy.30), calls=%async_computation.1 | async-start | bytes 1835008 | tf_op jit(solution)/shard_map/all_to_all | solution.py:80
  63.4 0.0 copy-done
  63.4 0.0 copy-done.2
  63.4 0.0 copy-start.1
  63.4 0.4 fusion.38
  63.8 0.0 copy-done.6
  63.8 0.1 iota_compare_fusion
  63.9 0.4 copy-done.1
  64.3 3.7 %fusion.14 = f32[2,128,2048]{2,1,0:T(8,128)S(1)} fusion(f32[2,128,2048]{2,1,0:T(8,128)S(1)} %fusion.38, bf16[2,128,512]{2,1,0:T(8,128)(2,1)S(1)} %copy-done.1, bf16[2,2048,512]{2,1,0:T(8,128)(2,1)} %param.19, pred[2,2048]{1,0:T(4,128)(4,1)S(1)} %iota_compare_fusion), kind=kOutput, calls=%fused_computation.15 | convolution fusion | flops 538443776 | bytes 8654848 | tf_op jit(solution)/shard_map/bhq,blq->bhl/dot_general | solution.py:24
  68.0 0.5 fusion.37
  68.5 3.9 %convolution_convert_fusion.1 = bf16[2,128,512]{2,1,0:T(8,128)(2,1)} fusion(bf16[2,2048,512]{2,1,0:T(8,128)(2,1)} %param.19, f32[2,128]{1,0:T(2,128)S(1)} %fusion.37, f32[2,128,2048]{2,1,0:T(8,128)S(1)} %fusion.14), kind=kOutput, calls=%fused_computation.17 | convolution fusion | flops 538577152 | bytes 6554624 | tf_op jit(solution)/shard_map/bhl,blq->bhq/dot_general | solution.py:36
  72.4 11.8 %all-to-all-done.1 = bf16[16,4,7168]{2,1,0:T(4,128)(2,1)S(1)} async-done(((bf16[16,4,7168]{2,1,0:T(4,128)(2,1)}), bf16[16,4,7168]{2,1,0:T(4,128)(2,1)S(1)}, u32[]{:S(2)}, u32[]{:S(2)}) %all-to-all-start.1) | async-done | bytes 917536 | tf_op jit(solution)/shard_map/all_to_all | solution.py:80
  84.2 0.5 bitcast_reduce_fusion
  84.7 1.1 %fusion.10 = bf16[4,7168]{1,0:T(4,128)(2,1)} fusion(bf16[8,4,7168]{2,1,0:T(4,128)(2,1)S(1)} %bitcast_reduce_fusion, f32[4,8]{1,0:T(4,128)S(1)} %select_reduce_fusion, s32[4,8]{1,0:T(4,128)S(1)} %sub.15, pred[4,8]{1,0:T(4,128)(4,1)S(1)} %broadcast_compare_fusion), kind=kOutput, calls=%fused_computation.10 | convolution fusion | flops 11039104 | bytes 516384 | tf_op jit(solution)/shard_map/tgc,gcd->td/dot_general | solution.py:86
  (4 shorter events, 0.1 us)
Async XLA Ops:
  0.6 62.7 %copy-start = (bf16[2,64,2048]{2,1,0:T(8,128)(2,1)S(1)}, bf16[2,64,2048]{2,1,0:T(8,128)(2,1)}, u32[]{:S(2)}) copy-start(bf16[2,64,2048]{2,1,0:T(8,128)(2,1)} %param.20) | copy-start | bytes 1572868
  2.7 9.2 %copy-start.3 = (bf16[2,8192]{1,0:T(2,128)(2,1)S(1)}, bf16[2,8192]{1,0:T(2,128)(2,1)}, u32[]{:S(2)}) copy-start(bf16[2,8192]{1,0:T(2,128)(2,1)} %param.18) | copy-start | bytes 98308
  2.7 9.9 %copy-start.4 = (s32[4,4]{1,0:T(4,128)S(1)}, s32[4,4]{1,0:T(4,128)}, u32[]{:S(2)}) copy-start(s32[4,4]{1,0:T(4,128)} %param.12) | copy-start | bytes 196
  2.7 9.9 %copy-start.5 = (f32[4,4]{1,0:T(4,128)S(1)}, f32[4,4]{1,0:T(4,128)}, u32[]{:S(2)}) copy-start(f32[4,4]{1,0:T(4,128)} %param.13) | copy-start | bytes 196
  4.3 38.1 %slice-start = ((s8[14680064]{0:T(1024)(128)(4,1)}), s8[2097152]{0:T(1024)(128)(4,1)S(1)}, s32[]{:S(2)}) async-start(s8[14680064]{0:T(1024)(128)(4,1)} %bitcast.35), calls=%async_computation.2 | async-start | bytes 4194304
  4.3 28.4 %all-to-all-start = ((bf16[16,4,7168]{2,1,0:T(4,128)(2,1)}), bf16[16,4,7168]{2,1,0:T(4,128)(2,1)}, u32[]{:S(2)}, u32[]{:S(2)}) async-start(bf16[16,4,7168]{2,1,0:T(4,128)(2,1)} %bitcast.1), calls=%async_computation | async-start | bytes 1835008 | tf_op jit(solution)/shard_map/all_to_all | solution.py:75
  34.4 8.0 %slice-start.1 = ((s8[14680064]{0:T(1024)(128)(4,1)}), s8[4194304]{0:T(1024)(128)(4,1)S(1)}, s32[]{:S(2)}) async-start(s8[14680064]{0:T(1024)(128)(4,1)} %bitcast.35), calls=%async_computation.3 | async-start | bytes 8388608
  34.4 8.0 %slice-start.2 = ((s8[14680064]{0:T(1024)(128)(4,1)}), s8[4194304]{0:T(1024)(128)(4,1)S(1)}, s32[]{:S(2)}) async-start(s8[14680064]{0:T(1024)(128)(4,1)} %bitcast.35), calls=%async_computation.4 | async-start | bytes 8388608
  34.5 8.8 %slice-start.3 = ((s8[14680064]{0:T(1024)(128)(4,1)}), s8[4194304]{0:T(1024)(128)(4,1)S(1)}, s32[]{:S(2)}) async-start(s8[14680064]{0:T(1024)(128)(4,1)} %bitcast.35), calls=%async_computation.5 | async-start | bytes 8388608
  55.4 8.0 %copy-start.2 = (bf16[2,128,64]{2,1,0:T(8,128)(2,1)S(1)}, bf16[2,128,64]{2,1,0:T(8,128)(2,1)}, u32[]{:S(2)}) copy-start(bf16[2,128,64]{2,1,0:T(8,128)(2,1)} %reshape.61) | copy-start | bytes 98308
  57.0 6.8 %copy-start.6 = (s32[2]{0:T(128)S(1)}, s32[2]{0:T(128)}, u32[]{:S(2)}) copy-start(s32[2]{0:T(128)} %param.21) | copy-start | bytes 28
  57.0 27.1 %all-to-all-start.1 = ((bf16[16,4,7168]{2,1,0:T(4,128)(2,1)}), bf16[16,4,7168]{2,1,0:T(4,128)(2,1)S(1)}, u32[]{:S(2)}, u32[]{:S(2)}) async-start(bf16[16,4,7168]{2,1,0:T(4,128)(2,1)} %copy.30), calls=%async_computation.1 | async-start | bytes 1835008 | tf_op jit(solution)/shard_map/all_to_all | solution.py:80
  63.4 1.0 %copy-start.1 = (bf16[2,128,512]{2,1,0:T(8,128)(2,1)S(1)}, bf16[2,128,512]{2,1,0:T(8,128)(2,1)}, u32[]{:S(2)}) copy-start(bf16[2,128,512]{2,1,0:T(8,128)(2,1)} %param.17) | copy-start | bytes 786436
where the time goes:
time: 87 us; the launch traced here: 85.8 us
  waiting for transfers between devices  31.9 us (37%)
  matrix products  29.3 us (34%)
  starting transfers between devices  13.9 us (16%)
  local copies, waits for them, and re-layouts  7.87 us (9%)
  other arithmetic  2.05 us (2%)
    all_to_all x1, waiting for transfers between devices, shards(): lax.all_to_all(spread, ('grp', 'loc'), split_axis=0, concat_axis=0, tiled...  20 us
    all_to_all x1, waiting for transfers between devices, shards(): lax.all_to_all(partial_value, ('grp', 'loc'), split_axis=0, concat_axis=0...  11.8 us
    dot_general x1, matrix products, expert_partial(): jnp.dot(flat_rows, gate_matrix, preferred_element_type=jnp.float32)  7.98 us
    dot_general x1, matrix products, expert_partial(): jnp.dot(hidden_act, down_matrix, preferred_element_type=jnp.float32)  7.84 us
    all_to_all x1, starting transfers between devices, shards(): lax.all_to_all(spread, ('grp', 'loc'), split_axis=0, concat_axis=0, tiled...  7.56 us
    all_to_all x1, starting transfers between devices, shards(): lax.all_to_all(partial_value, ('grp', 'loc'), split_axis=0, concat_axis=0...  6.32 us
    dot_general x1, matrix products, attend_local(): jnp.einsum('bhl,blq->bhq', weights, cache_latent, preferred_element_type=...  3.85 us
    dot_general x1, matrix products, attend_local(): jnp.einsum('bhq,blq->bhl', query_latent, cache_latent, preferred_element_...  3.7 us
  transfers between devices with their start and end apart: 2, of which 2 were waited for; matrix products, arithmetic and copies ran while one was open for 11% of the time, Pallas kernels for 0%

commit v1 on v0

v1 whole, which is shorter than its diff:
```python
import functools
import jax
import jax.numpy as jnp
from jax import lax
from jax.experimental import pallas as pl
from jax.experimental.pallas import tpu as pltpu
from jax.sharding import PartitionSpec as P

softmax_scale = 192.0 ** (-0.5)
mask_fill = -1e30
MESH = pl.DeviceIdType.MESH
EXT = 128
F32 = jnp.float32
BF16 = jnp.bfloat16


def fused(cfg, *refs):
    ng, nl, no, nh, kc, nc, pc = cfg
    (tok, picks, gsc, lens, qlat, qrope, wg_h, wu_h, wd_h, cl_h, cr_h,
     moe_out, attn_out,
     wg, wu, wd, cl, cr, sc, gat, x32, accg, accu, hs,
     sb1, rb1, sb2, rb2, sb3, rb3,
     wsem, dsem, csem, ghs, ghr, gos, gor, gls, glr,
     s1s, s1r, s2s, s2r, s3s, s3r) = refs
    tk, d = tok.shape
    hl = wg.shape[1]
    reqs, heads, lat = qlat.shape
    length = cl.shape[1]
    g = lax.axis_index("grp")
    l = lax.axis_index("loc")
    hi = g // no
    lo = g % no
    kstep = d // kc
    cw = d // nc

    cache_copies = []
    for r in range(reqs):
        pair = [pltpu.make_async_copy(cl_h.at[r], cl.at[r], csem.at[2 * r]),
                pltpu.make_async_copy(cr_h.at[r], cr.at[r], csem.at[2 * r + 1])]
        for c in pair:
            c.start()
        cache_copies.append(pair)
    w_copies = []
    for k in range(kc):
        rows = pl.ds(k * kstep, kstep)
        pair = [pltpu.make_async_copy(wg_h.at[0, rows], wg.at[rows], wsem.at[2 * k]),
                pltpu.make_async_copy(wu_h.at[0, rows], wu.at[rows], wsem.at[2 * k + 1])]
        for c in pair:
            c.start()
        w_copies.append(pair)
    d_copies = []
    for j in range(nc):
        cols = pl.ds(j * cw, cw)
        c = pltpu.make_async_copy(wd_h.at[0, :, cols], wd.at[:, cols], dsem.at[j])
        c.start()
        d_copies.append(c)

    def hi_dev(k):
        h2 = lax.rem(hi + k, nh)
        return h2, {"grp": h2 * no + lo, "loc": l}

    def lo_dev(k):
        o2 = lax.rem(lo + k, no)
        return o2, {"grp": hi * no + o2, "loc": l}

    def loc_dev(k):
        l2 = lax.rem(l + k, nl)
        return l2, {"grp": g, "loc": l2}

    lane = lax.broadcasted_iota(jnp.int32, (tk, EXT), 1)
    lane_g = lax.rem(lane, ng)
    weight = jnp.zeros((tk, EXT), F32)
    for k in range(picks.shape[1]):
        weight = weight + jnp.where(picks[:, k:k + 1] == lane_g, gsc[:, k:k + 1], 0.0)
    w1 = weight.astype(BF16).astype(F32)
    w2 = (weight - w1).astype(BF16).astype(F32)
    w3 = weight - w1 - w2
    terms = jnp.where(lane < ng, w1, jnp.where(lane < 2 * ng, w2, jnp.where(lane < 3 * ng, w3, 0.0)))
    gat[l, lo, hi, :, 0:d] = tok[...]
    gat[l, lo, hi, :, d:d + EXT] = terms.astype(BF16)

    barrier = pltpu.get_barrier_semaphore()
    peers = [hi_dev(k)[1] for k in range(1, nh)] + [lo_dev(k)[1] for k in range(1, no)] + [
        loc_dev(k)[1] for k in range(1, nl)]
    for dev in peers:
        pl.semaphore_signal(barrier, inc=1, device_id=dev, device_id_type=MESH)
    pl.semaphore_wait(barrier, len(peers))

    def remote(src, dst, ss, rs, dev):
        return pltpu.make_async_remote_copy(
            src_ref=src, dst_ref=dst, send_sem=ss, recv_sem=rs, device_id=dev, device_id_type=MESH)

    g_sends = []

    def go(copy):
        copy.start()
        g_sends.append(copy)

    mine = gat.at[l, lo, hi]
    for k in range(1, nh):
        go(remote(mine, mine, ghs.at[k], ghr.at[k], hi_dev(k)[1]))

    def forward(k):
        h2 = lax.rem(hi - k + nh, nh)
        blk = gat.at[l, lo, h2]
        if k > 0:
            remote(blk, blk, ghs.at[k], ghr.at[k], hi_dev(k)[1]).wait_recv()
        for m in range(1, no):
            go(remote(blk, blk, gos.at[m, k], gor.at[m, k], lo_dev(m)[1]))

    def loc_send(m):
        o2 = lax.rem(lo - m + no, no)
        if m > 0:
            for k in range(nh):
                blk = gat.at[l, o2, lax.rem(hi - k + nh, nh)]
                remote(blk, blk, gos.at[m, k], gor.at[m, k], lo_dev(m)[1]).wait_recv()
        part = gat.at[l, o2]
        for q in range(1, nl):
            go(remote(part, part, gls.at[q, m], glr.at[q, m], loc_dev(q)[1]))

    def loc_wait(m):
        o2 = lax.rem(lo - m + no, no)
        for q in range(1, nl):
            part = gat.at[lax.rem(l - q + nl, nl), o2]
            remote(part, part, gls.at[q, m], glr.at[q, m], loc_dev(q)[1]).wait_recv()

    forward(0)

    pw = length // pc

    def scores_of(r):
        for c in cache_copies[r]:
            c.wait()
        q = qlat[r]
        qr = qrope[r]
        top = None
        for b in range(pc):
            s = lax.dot_general(q, cl[r, b * pw:(b + 1) * pw, :], (((1,), (1,)), ((), ())),
                                preferred_element_type=F32)
            s = s + jnp.dot(qr, cr[r, :, b * pw:(b + 1) * pw], preferred_element_type=F32)
            pos = lax.broadcasted_iota(jnp.int32, (heads, pw), 1) + b * pw
            s = jnp.where(pos < lens[r], s * softmax_scale, mask_fill)
            sc[:, b * pw:(b + 1) * pw] = s
            t = jnp.max(s, axis=1, keepdims=True)
            top = t if top is None else jnp.maximum(top, t)
        return top

    def values_of(r, top):
        acc = jnp.zeros((heads, lat), F32)
        total = jnp.zeros((heads, 1), F32)
        for b in range(pc):
            p = jnp.exp(sc[:, b * pw:(b + 1) * pw] - top)
            total = total + jnp.sum(p, axis=1, keepdims=True)
            acc = acc + jnp.dot(p.astype(BF16), cl[r, b * pw:(b + 1) * pw, :],
                                preferred_element_type=F32)
        attn_out[r] = (acc / total).astype(BF16)

    units = []
    for r in range(reqs):
        box = {}
        units.append(lambda r=r, box=box: box.update(top=scores_of(r)))
        units.append(lambda r=r, box=box: values_of(r, box["top"]))
    steps = [functools.partial(forward, k) for k in range(1, nh)]
    steps.append(functools.partial(loc_send, 0))
    steps += [functools.partial(loc_send, m) for m in range(1, no)]
    order = [[] for _ in units]
    for i, s in enumerate(steps):
        order[min(i, len(units) - 1)].append(s)
    for unit, after in zip(units, order):
        unit()
        for s in after:
            s()
    for m in range(no):
        loc_wait(m)

    per = no * nh

    pack = max(1, 8 // tk)

    def put(i, _):
        parts = []
        for u in range(pack):
            at = i * pack + u
            rest = at % per
            parts.append(gat[at // per, rest // nh, rest % nh].astype(F32))
        x32[pl.ds(pl.multiple_of(i * (pack * tk), 8), pack * tk), :] = jnp.concatenate(parts, axis=0)
        return 0

    packs = nl * per // pack
    lax.fori_loop(0, packs, put, 0, unroll=min(8, packs))

    nt = min(256, hl)
    for k in range(kc):
        for c in w_copies[k]:
            c.wait()
        xk = x32[:, k * kstep:(k + 1) * kstep].astype(BF16)
        for n in range(hl // nt):
            cols = slice(n * nt, (n + 1) * nt)
            rows = slice(k * kstep, (k + 1) * kstep)
            pg = jnp.dot(xk, wg[rows, cols], preferred_element_type=F32)
            pu = jnp.dot(xk, wu[rows, cols], preferred_element_type=F32)
            if k > 0:
                pg = accg[:, cols] + pg
                pu = accu[:, cols] + pu
            if k < kc - 1:
                accg[:, cols] = pg
                accu[:, cols] = pu
            else:
                hs[:, cols] = (pg / (1.0 + jnp.exp(-pg)) * pu).astype(BF16)

    wlane = lax.broadcasted_iota(jnp.int32, (x32.shape[0], EXT), 1)
    hit = (lax.rem(wlane, ng) == g) & (wlane < 3 * ng)
    wcol = jnp.sum(jnp.where(hit, x32[:, d:d + EXT], 0.0), axis=1, keepdims=True)

    out_sends = []

    def send(copy):
        copy.start()
        out_sends.append(copy)

    def stage_m(j):
        d_copies[j].wait()
        y = jnp.dot(hs[...], wd[:, j * cw:(j + 1) * cw], preferred_element_type=F32) * wcol
        for i in range(nl * per):
            rest = i % per
            sb1[j, i // per, rest // nh, rest % nh] = y[i * tk:(i + 1) * tk].astype(BF16)
        for q in range(1, nl):
            l2, dev = loc_dev(q)
            send(remote(sb1.at[j, l2], rb1.at[j, q - 1], s1s.at[q, j], s1r.at[q, j], dev))

    def stage_a(j):
        z = sb1[j, l].astype(F32)
        for q in range(1, nl):
            remote(sb1.at[j, l], rb1.at[j, q - 1], s1s.at[q, j], s1r.at[q, j], loc_dev(q)[1]).wait_recv()
            z = z + rb1[j, q - 1].astype(F32)
        sb2[j] = z.astype(BF16)
        for m in range(1, no):
            o2, dev = lo_dev(m)
            send(remote(sb2.at[j, o2], rb2.at[j, m - 1], s2s.at[m, j], s2r.at[m, j], dev))

    def stage_b(j):
        z = sb2[j, lo].astype(F32)
        for m in range(1, no):
            remote(sb2.at[j, lo], rb2.at[j, m - 1], s2s.at[m, j], s2r.at[m, j], lo_dev(m)[1]).wait_recv()
            z = z + rb2[j, m - 1].astype(F32)
        sb3[j] = z.astype(BF16)
        for k in range(1, nh):
            h2, dev = hi_dev(k)
            send(remote(sb3.at[j, h2], rb3.at[j, k - 1], s3s.at[k, j], s3r.at[k, j], dev))

    def stage_c(j):
        z = sb3[j, hi].astype(F32)
        for k in range(1, nh):
            remote(sb3.at[j, hi], rb3.at[j, k - 1], s3s.at[k, j], s3r.at[k, j], hi_dev(k)[1]).wait_recv()
            z = z + rb3[j, k - 1].astype(F32)
        moe_out[:, j * cw:(j + 1) * cw] = z.astype(BF16)

    for s in range(nc + 7):
        for lag, stage in ((0, stage_m), (2, stage_a), (4, stage_b), (7, stage_c)):
            if 0 <= s - lag < nc:
                stage(s - lag)
    for c in g_sends + out_sends:
        c.wait_send()


def shards(moe_tokens, picked_groups, gate_scores, w_gate, w_up, w_down,
           query_latent, query_rope, cache_latent, cache_rope, cache_lengths):
    ng = lax.axis_size("grp")
    nl = lax.axis_size("loc")
    no = 2 if ng % 2 == 0 else 1
    nh = ng // no
    tk, d = moe_tokens.shape
    reqs, heads, lat = query_latent.shape
    rope, length = cache_rope.shape[1:]
    hl = w_gate.shape[2]
    kc, nc, pc = 4, 7, 4
    cw = d // nc
    rows = ng * nl * tk
    cfg = (ng, nl, no, nh, kc, nc, pc)
    vm = pl.BlockSpec(memory_space=pltpu.VMEM)
    sm = pl.BlockSpec(memory_space=pltpu.SMEM)
    hbm = pl.BlockSpec(memory_space=pl.ANY)
    dma = pltpu.SemaphoreType.DMA
    return tuple(pl.pallas_call(
        functools.partial(fused, cfg),
        out_shape=(jax.ShapeDtypeStruct((tk, d), BF16),
                   jax.ShapeDtypeStruct((reqs, heads, lat), BF16)),
        in_specs=[vm, vm, vm, sm, vm, vm] + [hbm] * 5,
        out_specs=(vm, vm),
        scratch_shapes=[
            pltpu.VMEM((d, hl), BF16), pltpu.VMEM((d, hl), BF16), pltpu.VMEM((hl, d), BF16),
            pltpu.VMEM((reqs, length, lat), BF16), pltpu.VMEM((reqs, rope, length), BF16),
            pltpu.VMEM((heads, length), F32),
            pltpu.VMEM((nl, no, nh, tk, d + EXT), BF16),
            pltpu.VMEM((rows, d + EXT), F32),
            pltpu.VMEM((rows, hl), F32), pltpu.VMEM((rows, hl), F32), pltpu.VMEM((rows, hl), BF16),
            pltpu.VMEM((nc, nl, no, nh, tk, cw), BF16), pltpu.VMEM((nc, nl - 1, no, nh, tk, cw), BF16),
            pltpu.VMEM((nc, no, nh, tk, cw), BF16), pltpu.VMEM((nc, no - 1, nh, tk, cw), BF16),
            pltpu.VMEM((nc, nh, tk, cw), BF16), pltpu.VMEM((nc, nh - 1, tk, cw), BF16),
            dma((2 * kc,)), dma((nc,)), dma((2 * reqs,)),
            dma((nh,)), dma((nh,)), dma((no, nh)), dma((no, nh)), dma((nl, no)), dma((nl, no)),
            dma((nl, nc)), dma((nl, nc)), dma((no, nc)), dma((no, nc)), dma((nh, nc)), dma((nh, nc)),
        ],
        compiler_params=pltpu.CompilerParams(
            collective_id=0, has_side_effects=True, vmem_limit_bytes=63 * 1024 * 1024),
    )(moe_tokens, picked_groups, gate_scores, cache_lengths, query_latent,
      query_rope.reshape(reqs, heads, rope), w_gate, w_up, w_down, cache_latent, cache_rope))


def solution(mesh):
    tokens = P(("rep", "grp", "loc"), None)
    requests = P(("rep", "grp", "loc"), None, None)
    placed = (
        tokens, tokens, tokens,
        P("grp", None, "loc"), P("grp", None, "loc"), P("grp", "loc", None),
        requests, tokens, requests, requests, P(("rep", "grp", "loc")),
    )
    return jax.shard_map(shards, mesh=mesh, in_specs=placed, out_specs=(tokens, requests),
                         check_vma=False)
```

time: 87 us -> 51.1 us (0.59); the launches traced: 85.8 us -> 50.8 us
  Pallas kernels: 0 us -> 45.6 us
  waiting for transfers between devices: 31.9 us -> 0 us
  matrix products: 29.3 us -> 0 us
  starting transfers between devices: 13.9 us -> 0 us
  local copies, waits for them, and re-layouts: 7.87 us -> 4.63 us
  other arithmetic: 2.05 us -> 0 us
    pallas_call x0 -> x1, Pallas kernels: none -> 45.6 us  [shards(): pl.pallas_call(functools.partial(fused, cfg), out_shape=(jax.ShapeDtypeSt...]
    all_to_all x2 -> x0, waiting for transfers between devices: 31.9 us -> none  [the longest x1 20 us: shards(): lax.all_to_all(spread, ('grp', 'loc'), split_axis=0, concat_axis=0, tiled...]
    dot_general x8 -> x0, matrix products: 29.3 us -> none  [the longest x1 7.98 us: expert_partial(): jnp.dot(flat_rows, gate_matrix, preferred_element_type=jnp.float32)]
    all_to_all x2 -> x0, starting transfers between devices: 13.9 us -> none  [the longest x1 7.56 us: shards(): lax.all_to_all(spread, ('grp', 'loc'), split_axis=0, concat_axis=0, tiled...]
    convert_element_type x2 -> x0, local copies, waits for them, and re-layouts: 2 us -> none  [the longest x1 1.64 us: shards(): partial_value = expert_partial(lax.all_to_all(spread, ('grp', 'loc'), spl...]
    unnamed x22 -> x2, local copies, waits for them, and re-layouts: 1.29 us -> 3.13 us
    reduce_sum x3 -> x0, other arithmetic: 1.46 us -> none  [the longest x1 0.83 us: shards(): chosen = jnp.sum(pick_hits.astype(jnp.int32), axis=1)]
    broadcast_in_dim x1 -> x0, local copies, waits for them, and re-layouts: 1.24 us -> none  [shards(): jnp.broadcast_to(send_rows[:, None], (groups, loc_count, tok_count, model...]
  transfers between devices with their start and end apart: 2 -> 0, of which waited for: 2 -> 0; matrix products, arithmetic and copies ran while one was open for 11% -> 0% of each run, Pallas kernels for 0% -> 0%
where the time goes in v1:
time: 51.1 us; the launch traced here: 50.8 us
  Pallas kernels  45.6 us (89%)
  local copies, waits for them, and re-layouts  4.63 us (9%)
  between operations  0.64 us (1%)
    pallas_call x1, Pallas kernels, shards(): pl.pallas_call(functools.partial(fused, cfg), out_shape=(jax.ShapeDtypeSt...  45.6 us
    unnamed x2, local copies, waits for them, and re-layouts  3.13 us
    reshape x1, local copies, waits for them, and re-layouts, shards(): query_rope.reshape(reqs, heads, rope)  1.5 us

profile of v1, /device:TPU:0, one launch (start us, length us, event | category | flops | bytes accessed | tf_op | source)
XLA Modules:
  0.0 50.8 jit_solution(1011421841269587146)
XLA Ops:
  0.6 1.5 %reshape.7.refs_5_ = bf16[2,128,64]{2,1,0:T(8,128)(2,1)} reshape(bf16[2,8192]{1,0:T(2,128)(2,1)} %param.18) | data formatting | bytes 65536 | tf_op jit(solution)/shard_map/reshape | solution.py:307
  2.1 45.6 %shard_map.122 = (bf16[4,7168]{1,0:T(4,128)(2,1)}, bf16[2,128,512]{2,1,0:T(8,128)(2,1)}) custom-call(bf16[4,7168]{1,0:T(4,128)(2,1)} %refs_0_.1, s32[4,4]{1,0:T(4,128)} %refs_1_.1, f32[4,4]{1,0:T(4,128)} %refs_2_.1, s32[2]{0:T(128)} %refs_3_.1, bf16[2,128,512]{2,1,0:T(8,128)(2,1)} %refs_4_.1, bf16[2,128,64]{2,1,0:T(8,128)(2,1)} %reshape.7.refs_5_, ...), custom_call_target="tpu_custom_call" | custom-call | tf_op jit(solution)/shard_map/pallas_call | solution.py:284
  47.7 1.5 %copy.15 = bf16[4,7168]{1,0:T(4,128)(2,1)} copy(bf16[4,7168]{1,0:T(4,128)(2,1)} %get-tuple-element.4) | data formatting | bytes 114688
  49.2 1.7 %copy.16 = bf16[2,128,512]{2,1,0:T(8,128)(2,1)} copy(bf16[2,128,512]{2,1,0:T(8,128)(2,1)} %get-tuple-element.5) | data formatting | bytes 524288

commit v2 on v1

--- a/solution.py
+++ b/solution.py
@@ -45,14 +45,11 @@
         rows = pl.ds(k * kstep, kstep)
         pair = [pltpu.make_async_copy(wg_h.at[0, rows], wg.at[rows], wsem.at[2 * k]),
                 pltpu.make_async_copy(wu_h.at[0, rows], wu.at[rows], wsem.at[2 * k + 1])]
-        for c in pair:
-            c.start()
         w_copies.append(pair)
     d_copies = []
     for j in range(nc):
         cols = pl.ds(j * cw, cw)
         c = pltpu.make_async_copy(wd_h.at[0, :, cols], wd.at[:, cols], dsem.at[j])
-        c.start()
         d_copies.append(c)
 
     def hi_dev(k):
@@ -125,16 +122,18 @@
             remote(part, part, gls.at[q, m], glr.at[q, m], loc_dev(q)[1]).wait_recv()
 
     forward(0)
+    for pair in w_copies:
+        for c in pair:
+            c.start()
+    for c in d_copies:
+        c.start()
 
     pw = length // pc
 
-    def scores_of(r):
-        for c in cache_copies[r]:
-            c.wait()
+    def scores_of(r, blocks, top):
         q = qlat[r]
         qr = qrope[r]
-        top = None
-        for b in range(pc):
+        for b in blocks:
             s = lax.dot_general(q, cl[r, b * pw:(b + 1) * pw, :], (((1,), (1,)), ((), ())),
                                 preferred_element_type=F32)
             s = s + jnp.dot(qr, cr[r, :, b * pw:(b + 1) * pw], preferred_element_type=F32)
@@ -145,31 +144,42 @@
             top = t if top is None else jnp.maximum(top, t)
         return top
 
-    def values_of(r, top):
-        acc = jnp.zeros((heads, lat), F32)
-        total = jnp.zeros((heads, 1), F32)
-        for b in range(pc):
+    def values_of(r, blocks, top, acc, total):
+        for b in blocks:
             p = jnp.exp(sc[:, b * pw:(b + 1) * pw] - top)
             total = total + jnp.sum(p, axis=1, keepdims=True)
             acc = acc + jnp.dot(p.astype(BF16), cl[r, b * pw:(b + 1) * pw, :],
                                 preferred_element_type=F32)
-        attn_out[r] = (acc / total).astype(BF16)
-
-    units = []
-    for r in range(reqs):
-        box = {}
-        units.append(lambda r=r, box=box: box.update(top=scores_of(r)))
-        units.append(lambda r=r, box=box: values_of(r, box["top"]))
+        return acc, total
+
     steps = [functools.partial(forward, k) for k in range(1, nh)]
     steps.append(functools.partial(loc_send, 0))
-    steps += [functools.partial(loc_send, m) for m in range(1, no)]
-    order = [[] for _ in units]
-    for i, s in enumerate(steps):
-        order[min(i, len(units) - 1)].append(s)
-    for unit, after in zip(units, order):
-        unit()
-        for s in after:
-            s()
+    half = pc // 2
+    halves = (range(0, half), range(half, pc))
+
+    def step():
+        if steps:
+            steps.pop(0)()
+
+    for r in range(reqs):
+        for c in cache_copies[r]:
+            c.wait()
+        top = scores_of(r, halves[0], None)
+        step()
+        top = scores_of(r, halves[1], top)
+        step()
+        acc, total = values_of(r, halves[0], top, jnp.zeros((heads, lat), F32), jnp.zeros((heads, 1), F32))
+        step()
+        if r == reqs - 1:
+            while steps:
+                step()
+            for m in range(1, no):
+                loc_send(m)
+        acc, total = values_of(r, halves[1], top, acc, total)
+        step()
+        attn_out[r] = (acc / total).astype(BF16)
+    while steps:
+        step()
     for m in range(no):
         loc_wait(m)
 

time: 51.1 us -> 45.6 us (0.89)
  Pallas kernels: 45.6 us -> 40.1 us
    pallas_call x1, Pallas kernels: 45.6 us -> 40.1 us  [shards(): pl.pallas_call(functools.partial(fused, cfg), out_shape=(jax.ShapeDtypeSt...]
where the time goes in v2:
time: 45.6 us; the launch traced here: 45.3 us
  Pallas kernels  40.1 us (88%)
  local copies, waits for them, and re-layouts  4.63 us (10%)
  between operations  0.64 us (1%)
    pallas_call x1, Pallas kernels, shards(): pl.pallas_call(functools.partial(fused, cfg), out_shape=(jax.ShapeDtypeSt...  40.1 us
    unnamed x2, local copies, waits for them, and re-layouts  3.13 us
    reshape x1, local copies, waits for them, and re-layouts, shards(): query_rope.reshape(reqs, heads, rope)  1.5 us

profile of v2, /device:TPU:0, one launch (start us, length us, event | category | flops | bytes accessed | tf_op | source)
XLA Modules:
  0.0 45.3 jit_solution(7673536499232007644)
XLA Ops:
  0.6 1.5 %reshape.7.refs_5_ = bf16[2,128,64]{2,1,0:T(8,128)(2,1)} reshape(bf16[2,8192]{1,0:T(2,128)(2,1)} %param.18) | data formatting | bytes 65536 | tf_op jit(solution)/shard_map/reshape | solution.py:317
  2.1 40.1 %shard_map.122 = (bf16[4,7168]{1,0:T(4,128)(2,1)}, bf16[2,128,512]{2,1,0:T(8,128)(2,1)}) custom-call(bf16[4,7168]{1,0:T(4,128)(2,1)} %refs_0_.1, s32[4,4]{1,0:T(4,128)} %refs_1_.1, f32[4,4]{1,0:T(4,128)} %refs_2_.1, s32[2]{0:T(128)} %refs_3_.1, bf16[2,128,512]{2,1,0:T(8,128)(2,1)} %refs_4_.1, bf16[2,128,64]{2,1,0:T(8,128)(2,1)} %reshape.7.refs_5_, ...), custom_call_target="tpu_custom_call" | custom-call | tf_op jit(solution)/shard_map/pallas_call | solution.py:294
  42.2 1.5 %copy.15 = bf16[4,7168]{1,0:T(4,128)(2,1)} copy(bf16[4,7168]{1,0:T(4,128)(2,1)} %get-tuple-element.4) | data formatting | bytes 114688
  43.7 1.7 %copy.16 = bf16[2,128,512]{2,1,0:T(8,128)(2,1)} copy(bf16[2,128,512]{2,1,0:T(8,128)(2,1)} %get-tuple-element.5) | data formatting | bytes 524288

commit v3 on v2

--- a/solution.py
+++ b/solution.py
@@ -125,8 +125,6 @@
     for pair in w_copies:
         for c in pair:
             c.start()
-    for c in d_copies:
-        c.start()
 
     pw = length // pc
 
@@ -164,6 +162,9 @@
     for r in range(reqs):
         for c in cache_copies[r]:
             c.wait()
+        if r == reqs - 1:
+            for c in d_copies:
+                c.start()
         top = scores_of(r, halves[0], None)
         step()
         top = scores_of(r, halves[1], top)
@@ -265,8 +266,8 @@
             z = z + rb3[j, k - 1].astype(F32)
         moe_out[:, j * cw:(j + 1) * cw] = z.astype(BF16)
 
-    for s in range(nc + 7):
-        for lag, stage in ((0, stage_m), (2, stage_a), (4, stage_b), (7, stage_c)):
+    for s in range(nc + 6):
+        for lag, stage in ((0, stage_m), (1, stage_a), (3, stage_b), (6, stage_c)):
             if 0 <= s - lag < nc:
                 stage(s - lag)
     for c in g_sends + out_sends:

time: 45.6 us -> 45.4 us (level)
  no operation moved by 1% of the time
where the time goes in v3:
time: 45.4 us; the launch traced here: 45.1 us
  Pallas kernels  39.8 us (88%)
  local copies, waits for them, and re-layouts  4.63 us (10%)
  between operations  0.64 us (1%)
    pallas_call x1, Pallas kernels, shards(): pl.pallas_call(functools.partial(fused, cfg), out_shape=(jax.ShapeDtypeSt...  39.8 us
    unnamed x2, local copies, waits for them, and re-layouts  3.13 us
    reshape x1, local copies, waits for them, and re-layouts, shards(): query_rope.reshape(reqs, heads, rope)  1.5 us

profile of v3, /device:TPU:0, one launch (start us, length us, event | category | flops | bytes accessed | tf_op | source)
XLA Modules:
  0.0 45.1 jit_solution(15499467807958677769)
XLA Ops:
  0.6 1.5 %reshape.7.refs_5_ = bf16[2,128,64]{2,1,0:T(8,128)(2,1)} reshape(bf16[2,8192]{1,0:T(2,128)(2,1)} %param.18) | data formatting | bytes 65536 | tf_op jit(solution)/shard_map/reshape | solution.py:318
  2.1 39.8 %shard_map.122 = (bf16[4,7168]{1,0:T(4,128)(2,1)}, bf16[2,128,512]{2,1,0:T(8,128)(2,1)}) custom-call(bf16[4,7168]{1,0:T(4,128)(2,1)} %refs_0_.1, s32[4,4]{1,0:T(4,128)} %refs_1_.1, f32[4,4]{1,0:T(4,128)} %refs_2_.1, s32[2]{0:T(128)} %refs_3_.1, bf16[2,128,512]{2,1,0:T(8,128)(2,1)} %refs_4_.1, bf16[2,128,64]{2,1,0:T(8,128)(2,1)} %reshape.7.refs_5_, ...), custom_call_target="tpu_custom_call" | custom-call | tf_op jit(solution)/shard_map/pallas_call | solution.py:295
  42.0 1.5 %copy.15 = bf16[4,7168]{1,0:T(4,128)(2,1)} copy(bf16[4,7168]{1,0:T(4,128)(2,1)} %get-tuple-element.4) | data formatting | bytes 114688
  43.4 1.7 %copy.16 = bf16[2,128,512]{2,1,0:T(8,128)(2,1)} copy(bf16[2,128,512]{2,1,0:T(8,128)(2,1)} %get-tuple-element.5) | data formatting | bytes 524288
